TPU v7x, 32 devices: a whole 2x2x4 slice. The times are simulated.
32 devices in a mesh: cast: 8 (over z, x), width: 2 (over y), thick: 2 (over core).
Axes of the slice: x: 2, y: 2, z: 4, core: 2. Of those that a mesh axis runs over, the one named last changes fastest.
Arguments:
- velocity: float32 [3, 64, 32, 256], P(None, 'cast', 'width', 'thick'), may hold values from -2 to 3.5
- magnetic: float32 [3, 64, 32, 256], P(None, 'cast', 'width', 'thick'), may hold values from -1.2 to 2.25
Outputs:
- updated_velocity: float32 [3, 64, 32, 256], P(None, 'cast', 'width', 'thick')
- potential: float32 [64, 32, 256], P('cast', 'width', 'thick')
All inputs are finite; a program needn't handle non-finite values.
Results may differ from a plain program's by a relative error of at most 0.0003.
Values sent between devices are 32-bit elements; how exact they have to be, the bound alone decides.
A program may use at most 64 MiB of HBM per device.

v0:
```python
import jax
import jax.numpy as jnp
from jax import lax
from jax.sharding import PartitionSpec as P

CYCLES = 2
SWEEPS = 3
LEVELS = 3


relax_weight = 0.8
section_weight = 0.5
cast_speed = 1.0


def padded_2(block, sides, width):
    for axis, dim in sides:
        count = lax.axis_size(axis)
        forward = [(i, i + 1) for i in range(count - 1)]
        backward = [(target, source) for source, target in forward]
        low = lax.ppermute(
            lax.slice_in_dim(block, block.shape[dim] - width, None, axis=dim), axis, forward
        )
        high = lax.ppermute(lax.slice_in_dim(block, 0, width, axis=dim), axis, backward)
        block = jnp.concatenate([low, block, high], axis=dim)
    return block


def shifted_sum(padded):
    total = padded[2:, 1:-1, 1:-1] + padded[:-2, 1:-1, 1:-1]
    total = total + padded[1:-1, 2:, 1:-1] + padded[1:-1, :-2, 1:-1]
    return total + padded[1:-1, 1:-1, 2:] + padded[1:-1, 1:-1, :-2]


def padded_potential(field):
    return padded_2(field, (("cast", 0), ("width", 1), ("thick", 2)), 1)


def operate(field):
    return 6.0 * field - shifted_sum(padded_potential(field))


def smooth_once(field, source):
    return field + relax_weight / 6.0 * (source - operate(field))


def smooth_group(field, source):
    for sweep_index in range(SWEEPS):
        field = smooth_once(field, source)
    return field


def restrict(residue):
    count_x, count_y, count_z = residue.shape
    blocks = residue.reshape(count_x // 2, 2, count_y // 2, 2, count_z // 2, 2)
    return 4.0 * jnp.mean(blocks, axis=(1, 3, 5))


def prolong(coarse):
    return jnp.repeat(jnp.repeat(jnp.repeat(coarse, 2, axis=0), 2, axis=1), 2, axis=2)


def coarse_solve(source):
    field = jnp.zeros(source.shape, jnp.float32)
    return smooth_group(field, source)


def vcycle(field, source, level):
    field = smooth_group(field, source)
    residue = source - operate(field)
    reduced = restrict(residue)
    if level + 1 == LEVELS - 1:
        coarse = coarse_solve(reduced)
    else:
        coarse = vcycle(jnp.zeros(reduced.shape, jnp.float32), reduced, level + 1)
    field = field + prolong(coarse)
    return smooth_group(field, source)


def cross(left, right):
    return jnp.stack(
        [
            left[1] * right[2] - left[2] * right[1],
            left[2] * right[0] - left[0] * right[2],
            left[0] * right[1] - left[1] * right[0],
        ],
        axis=0,
    )


def divergence(padded):
    total = padded[0, 2:, 1:-1, 1:-1] - padded[0, :-2, 1:-1, 1:-1]
    total = total + (padded[1, 1:-1, 2:, 1:-1] - padded[1, 1:-1, :-2, 1:-1])
    total = total + (padded[2, 1:-1, 1:-1, 2:] - padded[2, 1:-1, 1:-1, :-2])
    return 0.5 * total


def gradient(padded):
    return jnp.stack(
        [
            0.5 * (padded[2:, 1:-1, 1:-1] - padded[:-2, 1:-1, 1:-1]),
            0.5 * (padded[1:-1, 2:, 1:-1] - padded[1:-1, :-2, 1:-1]),
            0.5 * (padded[1:-1, 1:-1, 2:] - padded[1:-1, 1:-1, :-2]),
        ],
        axis=0,
    )


def per_device(velocity, magnetic):
    electric = cross(velocity, magnetic)
    padded_field = padded_2(electric, (("cast", 1), ("width", 2), ("thick", 3)), 1)
    source = -divergence(padded_field)
    potential = jnp.zeros(source.shape, jnp.float32)
    for cycle_index in range(CYCLES):
        potential = vcycle(potential, source, 0)
    current = electric - gradient(padded_potential(potential))
    force = cross(current, magnetic)
    moved = velocity + section_weight * force
    cells_total = float(moved[0].size * lax.axis_size(("cast", "width", "thick")))
    total = lax.psum(jnp.sum(moved[0]), ("cast", "width", "thick"))
    bulk = total / cells_total
    updated = jnp.concatenate([moved[:1] - bulk + cast_speed, moved[1:]], axis=0)
    return (updated, potential)


def solution(mesh):
    placed = (P(None, "cast", "width", "thick"), P(None, "cast", "width", "thick"))
    return jax.shard_map(
        per_device,
        mesh=mesh,
        in_specs=placed,
        out_specs=(P(None, "cast", "width", "thick"), P("cast", "width", "thick")),
        check_vma=False,
    )
```

profile of v0, /device:TPU:0, one launch (start us, length us, event | category | flops | bytes accessed | tf_op | source)
XLA Modules:
  0.0 766.0 jit_solution(4524341466969264552)
XLA Ops:
  1.9 5.5 collective-permute-start.7
  9.8 5.5 collective-permute-start.1
  16.6 4.5 collective-permute-start.9
  22.5 4.5 collective-permute-start.3
  40.0 5.5 collective-permute-start.13
  48.1 4.5 collective-permute-start.15
  54.0 5.4 collective-permute-start.31
  66.4 5.7 collective-permute-start.19
  76.1 4.5 collective-permute-start.21
  88.8 5.5 collective-permute-start.25
  96.9 4.5 collective-permute-start.27
  111.5 5.6 reshape.59
  121.0 5.5 collective-permute-start.37
  130.4 4.2 collective-permute-done.38
  141.3 5.7 collective-permute-start.43
  148.3 5.7 collective-permute-start.55
  157.1 4.2 collective-permute-done.44
  167.0 4.5 collective-permute-start.57
  173.0 5.4 collective-permute-start.49
  182.5 4.2 collective-permute-done.50
  197.6 5.4 collective-permute-start.61
  205.7 4.5 collective-permute-start.63
  218.1 5.7 collective-permute-start.67
  226.4 4.5 collective-permute-start.69
  239.2 5.7 collective-permute-start.73
  246.2 4.2 collective-permute-start.75
  262.6 5.7 collective-permute-start.79
  283.5 5.7 collective-permute-start.85
  304.9 5.7 collective-permute-start.91
  313.3 4.5 collective-permute-start.93
  326.0 5.7 collective-permute-start.97
  334.4 4.5 collective-permute-start.99
  347.2 5.7 collective-permute-start.103
  355.6 4.5 collective-permute-start.105
  368.3 5.7 collective-permute-start.109
  376.7 4.5 collective-permute-start.111
  389.5 5.7 collective-permute-start.115
  397.9 4.5 collective-permute-start.117
  410.6 5.7 collective-permute-start.121
  419.0 4.5 collective-permute-start.123
  431.8 5.7 collective-permute-start.127
  440.2 4.5 collective-permute-start.129
  451.6 5.6 reshape.67
  461.1 5.7 collective-permute-start.133
  468.1 4.2 collective-permute-start.135
  484.5 5.7 collective-permute-start.139
  505.4 5.7 collective-permute-start.145
  527.0 5.7 collective-permute-start.151
  535.3 4.5 collective-permute-start.153
  547.8 5.7 collective-permute-start.157
  556.1 4.5 collective-permute-start.159
  568.8 5.7 collective-permute-start.163
  575.9 4.2 collective-permute-start.165
  592.2 5.7 collective-permute-start.169
  613.2 5.7 collective-permute-start.175
  634.7 5.7 collective-permute-start.181
  643.1 4.5 collective-permute-start.183
  655.8 5.7 collective-permute-start.187
  664.2 4.5 collective-permute-start.189
  677.0 5.7 collective-permute-start.193
  685.4 4.5 collective-permute-start.195
  698.1 5.7 collective-permute-start.199
  706.5 4.5 collective-permute-start.201
  718.7 45.9 %psum.7 = f32[]{:T(128)} all-reduce(f32[]{:T(128)} %slice_reduce_fusion), channel_id=1, replica_groups=mesh['cast'=8,'width'=2,'thick'=2] {'cast','width','thick'}, use_global_device_ids=true, to_apply=%region_5.0 | all-reduce | flops 1 | bytes 8 | tf_op jit(solution)/shard_map/psum | solution.py:120
  (621 shorter events, 390.9 us)
Async XLA Ops:
  0.6 14.6 %collective-permute-start.6 = (f32[1,16,128]{2,1,0:T(8,128)S(1)}, f32[1,16,128]{2,1,0:T(8,128)S(1)}, u32[]{:S(2)}, u32[]{:S(2)}) collective-permute-start(f32[1,16,128]{2,1,0:T(8,128)S(1)} %broadcast.74), channel_id=1, source_target_pairs={{4,0},{8,4},{12,8},{16,12},{20,16},{24,20},{28,24},{5,1},{9,5},{13... | collective-permute-start | bytes 24584 | tf_op jit(solution)/shard_map/ppermute | solution.py:24
  1.9 13.3 %collective-permute-start.7 = (f32[1,16,128]{2,1,0:T(8,128)S(1)}, f32[1,16,128]{2,1,0:T(8,128)S(1)}, u32[]{:S(2)}, u32[]{:S(2)}) collective-permute-start(f32[1,16,128]{2,1,0:T(8,128)S(1)} %broadcast.74), channel_id=1, source_target_pairs={{0,4},{4,8},{8,12},{12,16},{16,20},{20,24},{24,28},{1,5},{5,9},{9,... | collective-permute-start | bytes 24584 | tf_op jit(solution)/shard_map/ppermute | solution.py:21
  8.5 12.7 %collective-permute-start = (f32[3,1,16,128]{3,2,1,0:T(8,128)S(1)}, f32[3,1,16,128]{3,2,1,0:T(8,128)S(1)}, u32[]{:S(2)}, u32[]{:S(2)}) collective-permute-start(f32[3,1,16,128]{3,2,1,0:T(8,128)S(1)} %get-tuple-element.28), channel_id=1, source_target_pairs={{4,0},{8,4},{12,8},{16,12},{20,16},{24,20},{28,24},{5,1},{9,5},{13... | collective-permute-start | bytes 73736 | tf_op jit(solution)/shard_map/ppermute | solution.py:24
  9.8 11.4 %collective-permute-start.1 = (f32[3,1,16,128]{3,2,1,0:T(8,128)S(1)}, f32[3,1,16,128]{3,2,1,0:T(8,128)S(1)}, u32[]{:S(2)}, u32[]{:S(2)}) collective-permute-start(f32[3,1,16,128]{3,2,1,0:T(8,128)S(1)} %get-tuple-element.27), channel_id=1, source_target_pairs={{0,4},{4,8},{8,12},{12,16},{16,20},{20,24},{24,28},{1,5},{5,9},{9,... | collective-permute-start | bytes 73736 | tf_op jit(solution)/shard_map/ppermute | solution.py:21
  15.3 11.8 %collective-permute-start.8 = (f32[10,1,128]{2,1,0:T(1,128)S(1)}, f32[10,1,128]{2,1,0:T(1,128)S(1)}, u32[]{:S(2)}, u32[]{:S(2)}) collective-permute-start(f32[10,1,128]{2,1,0:T(1,128)S(1)} %get-tuple-element.90), channel_id=1, source_target_pairs={{2,0},{3,1},{6,4},{7,5},{10,8},{11,9},{14,12},{15,13},{18,16},{19,... | collective-permute-start | bytes 15368 | tf_op jit(solution)/shard_map/ppermute | solution.py:24
  16.6 10.5 %collective-permute-start.9 = (f32[10,1,128]{2,1,0:T(1,128)S(1)}, f32[10,1,128]{2,1,0:T(1,128)S(1)}, u32[]{:S(2)}, u32[]{:S(2)}) collective-permute-start(f32[10,1,128]{2,1,0:T(1,128)S(1)} %get-tuple-element.89), channel_id=1, source_target_pairs={{0,2},{1,3},{4,6},{5,7},{8,10},{9,11},{12,14},{13,15},{16,18},{17,... | collective-permute-start | bytes 15368 | tf_op jit(solution)/shard_map/ppermute | solution.py:21
  28.7 9.8 %collective-permute-start.4 = (f32[3,10,18,1]{3,2,1,0:T(8,128)S(1)}, f32[3,10,18,1]{3,2,1,0:T(8,128)S(1)}, u32[]{:S(2)}, u32[]{:S(2)}) collective-permute-start(f32[3,10,18,1]{3,2,1,0:T(8,128)S(1)} %get-tuple-element.23), channel_id=1, source_target_pairs={{1,0},{3,2},{5,4},{7,6},{9,8},{11,10},{13,12},{15,14},{17,16},{19,... | collective-permute-start | bytes 6488 | tf_op jit(solution)/shard_map/ppermute | solution.py:24
  30.0 8.5 %collective-permute-start.5 = (f32[3,10,18,1]{3,2,1,0:T(8,128)S(1)}, f32[3,10,18,1]{3,2,1,0:T(8,128)S(1)}, u32[]{:S(2)}, u32[]{:S(2)}) collective-permute-start(f32[3,10,18,1]{3,2,1,0:T(8,128)S(1)} %get-tuple-element.24), channel_id=1, source_target_pairs={{0,1},{2,3},{4,5},{6,7},{8,9},{10,11},{12,13},{14,15},{16,17},{18,... | collective-permute-start | bytes 6488 | tf_op jit(solution)/shard_map/ppermute | solution.py:21
  46.8 12.6 %collective-permute-start.14 = (f32[10,1,128]{2,1,0:T(1,128)S(1)}, f32[10,1,128]{2,1,0:T(1,128)S(1)}, u32[]{:S(2)}, u32[]{:S(2)}) collective-permute-start(f32[10,1,128]{2,1,0:T(1,128)S(1)} %get-tuple-element.88), channel_id=1, source_target_pairs={{2,0},{3,1},{6,4},{7,5},{10,8},{11,9},{14,12},{15,13},{18,16},{19,... | collective-permute-start | bytes 15368 | tf_op jit(solution)/shard_map/ppermute | solution.py:24
  48.1 11.3 %collective-permute-start.15 = (f32[10,1,128]{2,1,0:T(1,128)S(1)}, f32[10,1,128]{2,1,0:T(1,128)S(1)}, u32[]{:S(2)}, u32[]{:S(2)}) collective-permute-start(f32[10,1,128]{2,1,0:T(1,128)S(1)} %get-tuple-element.87), channel_id=1, source_target_pairs={{0,2},{1,3},{4,6},{5,7},{8,10},{9,11},{12,14},{13,15},{16,18},{17,... | collective-permute-start | bytes 15368 | tf_op jit(solution)/shard_map/ppermute | solution.py:21
  52.7 11.3 %collective-permute-start.30 = (f32[1,8,64]{2,1,0:T(8,128)S(1)}, f32[1,8,64]{2,1,0:T(8,128)S(1)}, u32[]{:S(2)}, u32[]{:S(2)}) collective-permute-start(f32[1,8,64]{2,1,0:T(8,128)S(1)} %broadcast.78), channel_id=1, source_target_pairs={{4,0},{8,4},{12,8},{16,12},{20,16},{24,20},{28,24},{5,1},{9,5},{13... | collective-permute-start | bytes 6152 | tf_op jit(solution)/shard_map/ppermute | solution.py:24
  54.0 10.0 %collective-permute-start.31 = (f32[1,8,64]{2,1,0:T(8,128)S(1)}, f32[1,8,64]{2,1,0:T(8,128)S(1)}, u32[]{:S(2)}, u32[]{:S(2)}) collective-permute-start(f32[1,8,64]{2,1,0:T(8,128)S(1)} %broadcast.78), channel_id=1, source_target_pairs={{0,4},{4,8},{8,12},{12,16},{16,20},{20,24},{24,28},{1,5},{5,9},{9,... | collective-permute-start | bytes 6152 | tf_op jit(solution)/shard_map/ppermute | solution.py:21
  65.1 9.7 %collective-permute-start.18 = (f32[1,16,128]{2,1,0:T(8,128)S(1)}, f32[1,16,128]{2,1,0:T(8,128)S(1)}, u32[]{:S(2)}, u32[]{:S(2)}) collective-permute-start(f32[1,16,128]{2,1,0:T(8,128)S(1)} %get-tuple-element.116), channel_id=1, source_target_pairs={{4,0},{8,4},{12,8},{16,12},{20,16},{24,20},{28,24},{5,1},{9,5},{13... | collective-permute-start | bytes 24584 | tf_op jit(solution)/shard_map/ppermute | solution.py:24
  66.4 8.4 %collective-permute-start.19 = (f32[1,16,128]{2,1,0:T(8,128)S(1)}, f32[1,16,128]{2,1,0:T(8,128)S(1)}, u32[]{:S(2)}, u32[]{:S(2)}) collective-permute-start(f32[1,16,128]{2,1,0:T(8,128)S(1)} %get-tuple-element.115), channel_id=1, source_target_pairs={{0,4},{4,8},{8,12},{12,16},{16,20},{20,24},{24,28},{1,5},{5,9},{9,... | collective-permute-start | bytes 24584 | tf_op jit(solution)/shard_map/ppermute | solution.py:21
  72.1 8.5 %collective-permute-start.33 = (f32[6,1,64]{2,1,0:T(1,128)S(1)}, f32[6,1,64]{2,1,0:T(1,128)S(1)}, u32[]{:S(2)}, u32[]{:S(2)}) collective-permute-start(f32[6,1,64]{2,1,0:T(1,128)S(1)} %get-tuple-element.196), channel_id=1, source_target_pairs={{0,2},{1,3},{4,6},{5,7},{8,10},{9,11},{12,14},{13,15},{16,18},{17,... | collective-permute-start | bytes 4616 | tf_op jit(solution)/shard_map/ppermute | solution.py:21
  73.4 20.9 %collective-permute-start.32 = (f32[6,1,64]{2,1,0:T(1,128)S(1)}, f32[6,1,64]{2,1,0:T(1,128)S(1)}, u32[]{:S(2)}, u32[]{:S(2)}) collective-permute-start(f32[6,1,64]{2,1,0:T(1,128)S(1)} %get-tuple-element.195), channel_id=1, source_target_pairs={{2,0},{3,1},{6,4},{7,5},{10,8},{11,9},{14,12},{15,13},{18,16},{19,... | collective-permute-start | bytes 4616 | tf_op jit(solution)/shard_map/ppermute | solution.py:24
  95.6 10.3 %collective-permute-start.26 = (f32[10,1,128]{2,1,0:T(1,128)S(1)}, f32[10,1,128]{2,1,0:T(1,128)S(1)}, u32[]{:S(2)}, u32[]{:S(2)}) collective-permute-start(f32[10,1,128]{2,1,0:T(1,128)S(1)} %get-tuple-element.84), channel_id=1, source_target_pairs={{2,0},{3,1},{6,4},{7,5},{10,8},{11,9},{14,12},{15,13},{18,16},{19,... | collective-permute-start | bytes 15368 | tf_op jit(solution)/shard_map/ppermute | solution.py:24
  96.9 9.0 %collective-permute-start.27 = (f32[10,1,128]{2,1,0:T(1,128)S(1)}, f32[10,1,128]{2,1,0:T(1,128)S(1)}, u32[]{:S(2)}, u32[]{:S(2)}) collective-permute-start(f32[10,1,128]{2,1,0:T(1,128)S(1)} %get-tuple-element.83), channel_id=1, source_target_pairs={{0,2},{1,3},{4,6},{5,7},{8,10},{9,11},{12,14},{13,15},{16,18},{17,... | collective-permute-start | bytes 15368 | tf_op jit(solution)/shard_map/ppermute | solution.py:21
  101.6 8.8 %collective-permute-start.34 = (f32[6,10,1]{2,0,1:T(8,128)S(1)}, f32[6,10,1]{2,0,1:T(8,128)S(1)}, u32[]{:S(2)}, u32[]{:S(2)}) collective-permute-start(f32[6,10,1]{2,0,1:T(8,128)S(1)} %get-tuple-element.169), channel_id=1, source_target_pairs={{1,0},{3,2},{5,4},{7,6},{9,8},{11,10},{13,12},{15,14},{17,16},{19,... | collective-permute-start | bytes 728 | tf_op jit(solution)/shard_map/ppermute | solution.py:24
  102.9 7.5 collective-permute-start.35
  140.0 14.1 %collective-permute-start.42 = (f32[1,8,64]{2,1,0:T(8,128)S(1)}, f32[1,8,64]{2,1,0:T(8,128)S(1)}, u32[]{:S(2)}, u32[]{:S(2)}) collective-permute-start(f32[1,8,64]{2,1,0:T(8,128)S(1)} %get-tuple-element.228), channel_id=1, source_target_pairs={{4,0},{8,4},{12,8},{16,12},{20,16},{24,20},{28,24},{5,1},{9,5},{13... | collective-permute-start | bytes 6152 | tf_op jit(solution)/shard_map/ppermute | solution.py:24
  141.3 12.8 %collective-permute-start.43 = (f32[1,8,64]{2,1,0:T(8,128)S(1)}, f32[1,8,64]{2,1,0:T(8,128)S(1)}, u32[]{:S(2)}, u32[]{:S(2)}) collective-permute-start(f32[1,8,64]{2,1,0:T(8,128)S(1)} %get-tuple-element.227), channel_id=1, source_target_pairs={{0,4},{4,8},{8,12},{12,16},{16,20},{20,24},{24,28},{1,5},{5,9},{9,... | collective-permute-start | bytes 6152 | tf_op jit(solution)/shard_map/ppermute | solution.py:21
  147.0 8.7 %collective-permute-start.54 = (f32[1,4,32]{2,1,0:T(4,128)S(1)}, f32[1,4,32]{2,1,0:T(4,128)S(1)}, u32[]{:S(2)}, u32[]{:S(2)}) collective-permute-start(f32[1,4,32]{2,1,0:T(4,128)S(1)} %broadcast.82), channel_id=1, source_target_pairs={{4,0},{8,4},{12,8},{16,12},{20,16},{24,20},{28,24},{5,1},{9,5},{13... | collective-permute-start | bytes 1544 | tf_op jit(solution)/shard_map/ppermute | solution.py:24
  148.3 7.4 collective-permute-start.55
  161.3 10.2 %collective-permute-start.46 = (f32[6,10,1]{2,0,1:T(8,128)S(1)}, f32[6,10,1]{2,0,1:T(8,128)S(1)}, u32[]{:S(2)}, u32[]{:S(2)}) collective-permute-start(f32[6,10,1]{2,0,1:T(8,128)S(1)} %get-tuple-element.161), channel_id=1, source_target_pairs={{1,0},{3,2},{5,4},{7,6},{9,8},{11,10},{13,12},{15,14},{17,16},{19,... | collective-permute-start | bytes 728 | tf_op jit(solution)/shard_map/ppermute | solution.py:24
  162.6 8.9 %collective-permute-start.47 = (f32[6,10,1]{2,0,1:T(8,128)S(1)}, f32[6,10,1]{2,0,1:T(8,128)S(1)}, u32[]{:S(2)}, u32[]{:S(2)}) collective-permute-start(f32[6,10,1]{2,0,1:T(8,128)S(1)} %get-tuple-element.162), channel_id=1, source_target_pairs={{0,1},{2,3},{4,5},{6,7},{8,9},{10,11},{12,13},{14,15},{16,17},{18,... | collective-permute-start | bytes 728 | tf_op jit(solution)/shard_map/ppermute | solution.py:21
  165.7 12.8 %collective-permute-start.56 = (f32[4,1,32]{2,1,0:T(1,128)S(1)}, f32[4,1,32]{2,1,0:T(1,128)S(1)}, u32[]{:S(2)}, u32[]{:S(2)}) collective-permute-start(f32[4,1,32]{2,1,0:T(1,128)S(1)} %get-tuple-element.240), channel_id=1, source_target_pairs={{2,0},{3,1},{6,4},{7,5},{10,8},{11,9},{14,12},{15,13},{18,16},{19,... | collective-permute-start | bytes 1544 | tf_op jit(solution)/shard_map/ppermute | solution.py:24
  167.0 11.5 %collective-permute-start.57 = (f32[4,1,32]{2,1,0:T(1,128)S(1)}, f32[4,1,32]{2,1,0:T(1,128)S(1)}, u32[]{:S(2)}, u32[]{:S(2)}) collective-permute-start(f32[4,1,32]{2,1,0:T(1,128)S(1)} %get-tuple-element.239), channel_id=1, source_target_pairs={{0,2},{1,3},{4,6},{5,7},{8,10},{9,11},{12,14},{13,15},{16,18},{17,... | collective-permute-start | bytes 1544 | tf_op jit(solution)/shard_map/ppermute | solution.py:21
  186.7 8.7 %collective-permute-start.52 = (f32[6,10,1]{2,0,1:T(8,128)S(1)}, f32[6,10,1]{2,0,1:T(8,128)S(1)}, u32[]{:S(2)}, u32[]{:S(2)}) collective-permute-start(f32[6,10,1]{2,0,1:T(8,128)S(1)} %get-tuple-element.157), channel_id=1, source_target_pairs={{1,0},{3,2},{5,4},{7,6},{9,8},{11,10},{13,12},{15,14},{17,16},{19,... | collective-permute-start | bytes 728 | tf_op jit(solution)/shard_map/ppermute | solution.py:24
  188.0 7.4 collective-permute-start.53
  237.9 7.0 collective-permute-start.72
  239.2 7.0 collective-permute-start.73
  261.3 7.0 collective-permute-start.78
  262.6 7.0 collective-permute-start.79
  283.5 7.0 collective-permute-start.85
  304.9 7.1 collective-permute-start.91
  324.7 7.0 collective-permute-start.96
  326.0 7.1 collective-permute-start.97
  345.9 7.0 collective-permute-start.102
  347.2 7.1 collective-permute-start.103
  367.0 7.0 collective-permute-start.108
  368.3 7.1 collective-permute-start.109
  388.2 7.0 collective-permute-start.114
  389.5 7.1 collective-permute-start.115
  409.3 7.0 collective-permute-start.120
  410.6 7.1 collective-permute-start.121
  430.5 7.0 collective-permute-start.126
  431.8 7.1 collective-permute-start.127
  459.8 7.0 collective-permute-start.132
  461.1 7.0 collective-permute-start.133
  484.5 7.0 collective-permute-start.139
  505.4 7.0 collective-permute-start.145
  567.5 7.0 collective-permute-start.162
  568.8 7.0 collective-permute-start.163
  590.9 7.0 collective-permute-start.168
  592.2 7.0 collective-permute-start.169
  613.2 7.0 collective-permute-start.175
  634.7 7.1 collective-permute-start.181
  654.5 7.0 collective-permute-start.186
  655.8 7.1 collective-permute-start.187
  675.7 7.0 collective-permute-start.192
  677.0 7.1 collective-permute-start.193
  696.8 7.0 collective-permute-start.198
  698.1 7.1 collective-permute-start.199
  (143 other events, 954.4 us)
where the time goes:
time: 771 us; the launch traced here: 766 us
  starting transfers between devices  551 us (71%)
  waiting for transfers between devices  134 us (17%)
  blocking collectives  45.9 us (6%)
  local copies, waits for them, and re-layouts  16.8 us (2%)
  other arithmetic  12.8 us (2%)
    ppermute x102, starting transfers between devices, padded_2(): lax.ppermute(lax.slice_in_dim(block, block.shape[dim] - width, None, axis...  419 us
    ppermute x102, starting transfers between devices, padded_2(): lax.ppermute(lax.slice_in_dim(block, 0, width, axis=dim), axis, backward)  132 us
    ppermute x102, waiting for transfers between devices, padded_2(): lax.ppermute(lax.slice_in_dim(block, block.shape[dim] - width, None, axis...  84.3 us
    ppermute x102, waiting for transfers between devices, padded_2(): lax.ppermute(lax.slice_in_dim(block, 0, width, axis=dim), axis, backward)  50.1 us
    psum x1, blocking collectives, per_device(): total = lax.psum(jnp.sum(moved[0]), ('cast', 'width', 'thick'))  45.9 us
  transfers between devices with their start and end apart: 204, of which 86 were waited for; matrix products, arithmetic and copies ran while one was open for 0% of the time, Pallas kernels for 0%

commit v1 on v0

v1 whole, which is shorter than its diff:
```python
import functools

import jax
import jax.numpy as jnp
from jax import lax
from jax.experimental import pallas as pl
from jax.experimental.pallas import tpu as pltpu
from jax.sharding import PartitionSpec as P

CYCLES = 2
weight = 0.8 / 6.0
keep = 0.2
section_weight = 0.5
cast_speed = 1.0
HIGH = lax.Precision.HIGHEST
MESH = pl.DeviceIdType.MESH

HALO0 = 12
NEAR = 4


def dot(a, b):
    return jnp.dot(a, b, precision=HIGH, preferred_element_type=jnp.float32)


def iotas(shape):
    return lax.broadcasted_iota(jnp.int32, shape, 0), lax.broadcasted_iota(jnp.int32, shape, 1)


def pair_matrix(rows, cols, fine_axis, offset=0):
    i, j = iotas((rows, cols))
    if fine_axis == 0:
        hit = lax.shift_right_logical(i, 1) + offset == j
    else:
        hit = lax.shift_right_logical(j, 1) == i
    return jnp.where(hit, 1.0, 0.0).astype(jnp.float32)


def kernel(
    counts, v_ref, b_ref, out_ref, pot_ref,
    e_ref, sblk, exl, exr, eys, eyn, ezp,
    gk, fa, fb, g1blk, g1w, f1a, f1b, r1, g2, f2a, f2b,
    s1, s2, part1, part2,
    sem_as, sem_ar, sem_bs, sem_br, sem_cs, sem_cr, sem_ps, sem_pr, sem_loc,
):
    CX, CW = counts
    X, Y, Z = sblk.shape
    Y0, Z0 = gk.shape[1], gk.shape[2]
    Y1, Y2 = g1w.shape[2], g2.shape[1]
    two = CW == 2
    c, w, t = lax.axis_index("cast"), lax.axis_index("width"), lax.axis_index("thick")
    nx0 = CX * X

    def has_x(d):
        return jnp.logical_and(c + d >= 0, c + d < CX)

    def has_w(d):
        return jnp.logical_and(w + d >= 0, w + d < CW)

    def dys(reach):
        return (0, 1) if two else tuple(range(-reach, reach + 1))

    def wid(dy):
        return lax.rem(w + dy, 2) if two else w + dy

    def when_x(dx, fn):
        if dx == 0:
            fn()
        else:
            pl.when(has_x(dx))(fn)

    def when_w(dy, fn):
        if dy == 0 or two:
            fn()
        else:
            pl.when(has_w(dy))(fn)

    for ref in (exl, exr, eyn):
        ref[...] = jnp.zeros_like(ref)

    def clear(ref, first, count, per):
        def body(i, carry):
            for j in range(per):
                ref[first + i * per + j] = jnp.zeros(ref.shape[1:], jnp.float32)
            return carry

        lax.fori_loop(0, count // per, body, 0)

    if two:
        @pl.when(jnp.logical_not(has_x(-2)))
        def _():
            clear(gk, 0, 4, 4)

        @pl.when(jnp.logical_not(has_x(-1)))
        def _():
            clear(gk, 4, 8, 4)

        @pl.when(jnp.logical_not(has_x(1)))
        def _():
            clear(gk, 20, 8, 4)

        @pl.when(jnp.logical_not(has_x(2)))
        def _():
            clear(gk, 28, 4, 4)

        for n in range(CYCLES):
            for dx in range(-NEAR, NEAR + 1):
                if dx:
                    @pl.when(jnp.logical_not(has_x(dx)))
                    def _(n=n, dx=dx):
                        clear(g1w.at[n], 4 * (NEAR + dx), 4, 4)
    else:
        clear(gk, 0, gk.shape[0], 4)
        for n in range(CYCLES):
            clear(g1w.at[n], 0, g1w.shape[1], 4)

    barrier = pltpu.get_barrier_semaphore()
    need = jnp.int32(CX - 1)
    for d in range(1, CX):
        pl.semaphore_signal(barrier, 1, device_id=(lax.rem(c + d, CX), w, t), device_id_type=MESH)
    all_w = (0, 1) if two else tuple(range(-(CW - 1), CW))
    far = NEAR
    for dx in range(-far, far + 1):
        for dy in all_w:
            for dt in (0, 1):
                if dy == 0 and dt == 0:
                    continue
                wide = abs(dx) <= 2 and (two or abs(dy) <= 1)
                coarse = dt == 0 and (two or abs(dy) <= 2)
                if not (wide or coarse or dx == 0):
                    continue
                ok = jnp.bool_(True)
                if dx:
                    ok = jnp.logical_and(ok, has_x(dx))
                if dy and not two:
                    ok = jnp.logical_and(ok, has_w(dy))

                def greet(dx=dx, dy=dy, dt=dt):
                    pl.semaphore_signal(
                        barrier, 1, device_id=(c + dx, wid(dy), lax.rem(t + dt, 2)), device_id_type=MESH
                    )

                if dx == 0 and (dy == 0 or two):
                    greet()
                    need = need + 1
                else:
                    pl.when(ok)(greet)
                    need = need + jnp.where(ok, 1, 0).astype(jnp.int32)

    for i in range(X):
        v0, v1, v2 = v_ref[0, i], v_ref[1, i], v_ref[2, i]
        b0, b1, b2 = b_ref[0, i], b_ref[1, i], b_ref[2, i]
        e_ref[0, i] = v1 * b2 - v2 * b1
        ey = v2 * b0 - v0 * b2
        e_ref[1, i] = ey
        eys[0, i : i + 1, :] = ey[0:1, :]
        eys[1, i : i + 1, :] = ey[Y - 1 : Y, :]
        e_ref[2, i] = v0 * b1 - v1 * b0

    pl.semaphore_wait(barrier, need)

    def copy_a(k):
        if k == 0:
            args = (e_ref.at[0, X - 1], exl, (c + 1, w, t))
        elif k == 1:
            args = (e_ref.at[0, 0], exr, (c - 1, w, t))
        elif k == 2:
            args = (eys.at[1], eyn.at[0], (c, w + 1, t))
        elif k == 3:
            args = (eys.at[0], eyn.at[1], (c, w - 1, t))
        else:
            args = (e_ref.at[2], ezp, (c, w, 1 - t))
        return pltpu.make_async_remote_copy(
            args[0], args[1], sem_as.at[k], sem_ar.at[k], device_id=args[2], device_id_type=MESH
        )

    send_ok = (has_x(1), has_x(-1), has_w(1), has_w(-1))
    recv_ok = (has_x(-1), has_x(1), has_w(-1), has_w(1))
    for k in range(4):
        pl.when(send_ok[k])(lambda k=k: copy_a(k).start())
    copy_a(4).start()
    for k in range(4):
        pl.when(recv_ok[k])(lambda k=k: copy_a(k).wait_recv())
    copy_a(4).wait_recv()

    row, lane = iotas((Y, Z))
    for i in range(X):
        ex0 = e_ref[0, i - 1] if i else exl[...]
        ex1 = e_ref[0, i + 1] if i < X - 1 else exr[...]
        ey, ez, pz = e_ref[1, i], e_ref[2, i], ezp[i]
        ey1 = jnp.where(row == Y - 1, eyn[1, i : i + 1, :], pltpu.roll(ey, Y - 1, 0))
        ey0 = jnp.where(row == 0, eyn[0, i : i + 1, :], pltpu.roll(ey, 1, 0))
        edge1 = jnp.where(t == 0, pltpu.roll(pz, Z - 1, 1), 0.0)
        edge0 = jnp.where(t == 0, 0.0, pltpu.roll(pz, 1, 1))
        ez1 = jnp.where(lane == Z - 1, edge1, pltpu.roll(ez, Z - 1, 1))
        ez0 = jnp.where(lane == 0, edge0, pltpu.roll(ez, 1, 1))
        sblk[i] = (-0.5 * weight) * ((ex1 - ex0) + (ey1 - ey0) + (ez1 - ez0))

    def rows_b(dy):
        return pl.ds(pl.multiple_of(w * Y, Y), Y) if two else pl.ds((1 - dy) * Y, Y)

    my_lanes = pl.ds(pl.multiple_of(t * Z, Z), Z)
    ydys = dys(1)

    def copy_b(dx, dy, dt):
        if dx == 2:
            src, dst = (4, 4), 0
        elif dx == -2:
            src, dst = (0, 4), HALO0 + X + X
        else:
            src, dst = (0, X), HALO0 - dx * X
        k = ((dx + 2) * len(ydys) + ydys.index(dy)) * 2 + dt
        return pltpu.make_async_remote_copy(
            sblk.at[pl.ds(src[0], src[1])],
            gk.at[pl.ds(dst, src[1]), rows_b(dy), my_lanes],
            sem_bs.at[k], sem_br.at[k],
            device_id=(c + dx, wid(dy), lax.rem(t + dt, 2)), device_id_type=MESH,
        )

    def each_b(fn, sign):
        for dx in (1, -1, 2, -2, 0):
            def run(dx=dx):
                for dy in ydys:
                    def run_w(dy=dy):
                        for dt in (0, 1):
                            if dx or dy or dt:
                                fn(copy_b(dx, dy, dt))

                    if two:
                        run_w()
                    else:
                        when_w(sign * dy, run_w)

            when_x(sign * dx, run)

    each_b(lambda d: d.start(), 1)
    own = pltpu.make_async_copy(
        sblk, gk.at[pl.ds(HALO0, X), pl.ds(pl.multiple_of(w * Y, Y), Y) if two else pl.ds(Y, Y), my_lanes],
        sem_loc.at[0],
    )
    own.start()
    own.wait()
    each_b(lambda d: d.wait_recv(), -1)

    def neighbours(v):
        ny, nz = v.shape
        r, l = iotas(v.shape)
        total = jnp.where(r == 0, 0.0, pltpu.roll(v, 1, 0)) + jnp.where(r == ny - 1, 0.0, pltpu.roll(v, ny - 1, 0))
        total = total + jnp.where(l == 0, 0.0, pltpu.roll(v, 1, 1))
        return total + jnp.where(l == nz - 1, 0.0, pltpu.roll(v, nz - 1, 1))

    def factor(plane, first, count, shape, lev):
        g = first + plane
        k = jnp.where(jnp.logical_and(g >= 0, g < count), weight, 0.0).astype(jnp.float32)
        if not two:
            base = (w * Y - Y, w * (Y // 2) - Y, w * (Y // 4) - Y // 2)[lev]
            size = (CW * Y, CW * (Y // 2), CW * (Y // 4))[lev]
            r, _ = iotas(shape)
            k = jnp.where(jnp.logical_and(r + base >= 0, r + base < size), k, 0.0)
        if lev == 2:
            _, l = iotas(shape)
            k = jnp.where(l < Z0 // 4, k, 0.0)
        return k

    def apply(lev, src, g, dst, lo, hi, residual=False, last=None):
        first = (c * X - HALO0, c * (X // 2) - NEAR * (X // 2), c * (X // 4) - NEAR * (X // 4))[lev]
        count = nx0 >> lev
        n = hi - lo
        step = max(d for d in ((1, 2) if lev == 0 else (1, 2, 3, 4, 5)) if n % d == 0)

        def body(i, carry):
            p = lo + i * step
            v = [src[p - 1 + j] for j in range(step + 2)]
            for j in range(step):
                mid = v[j + 1]
                nb = v[j] + v[j + 2] + neighbours(mid)
                k = factor(p + j, first, count, mid.shape, lev)
                if residual:
                    dst[p + j] = g[p + j] + k * nb - 0.8 * mid
                else:
                    dst[p + j] = keep * mid + k * nb + g[p + j]
            return carry

        lax.fori_loop(0, n // step, body, 0)

    def own_rows(v):
        return jnp.where(w == 0, v[:Y], v[Y:]) if two else v[Y : 2 * Y]

    def own_lanes(v):
        return jnp.where(t == 0, v[:, :Z], v[:, Z:])

    H1 = NEAR * (X // 2)
    H2 = NEAR * (X // 4)
    pz0 = pair_matrix(Z0, Z0 // 2, 0)
    pz1 = pair_matrix(Z0 // 2, Z0 // 2, 0)
    uz0 = pair_matrix(Z0 // 2, Z0, 1)
    uz1 = pair_matrix(Z0 // 2, Z0 // 2, 1)
    py0 = pair_matrix(Y // 2, Y, 1)
    py1 = pair_matrix(Y2, Y1, 1)
    uy1 = pair_matrix(Y1, Y2, 0)
    uy0 = pair_matrix(Y0, Y1, 0, 0 if two else Y // 2)

    cdys = dys(2)

    def rows_c(dy):
        half = Y // 2
        return pl.ds(pl.multiple_of(w * half, half), half) if two else pl.ds((2 - dy) * half, half)

    def copy_c(n, dx, dy):
        k = (dx + NEAR) * len(cdys) + cdys.index(dy)
        return pltpu.make_async_remote_copy(
            g1blk.at[n], g1w.at[n, pl.ds((NEAR - dx) * (X // 2), X // 2), rows_c(dy)],
            sem_cs.at[n, k], sem_cr.at[n, k],
            device_id=(c + dx, wid(dy), t), device_id_type=MESH,
        )

    def each_c(n, fn, sign):
        for dx in (4, -4, 3, -3, 2, -2, 1, -1, 0):
            def run(dx=dx):
                for dy in cdys:
                    if dx or dy:
                        when_w(sign * dy, lambda dy=dy: fn(copy_c(n, dx, dy)))

            when_x(sign * dx, run)

    def coarse(n, src, out0):
        apply(0, src, gk, fb, HALO0, HALO0 + X, residual=True)
        sums = [own_rows(fb[HALO0 + 2 * i] + fb[HALO0 + 2 * i + 1]) for i in range(X // 2)]
        flat = 0.5 * dot(jnp.concatenate(sums, axis=0), pz0)
        for i in range(X // 2):
            g1blk[n, i] = dot(py0, flat[i * Y : (i + 1) * Y])
        each_c(n, lambda d: d.start(), 1)
        mine = pltpu.make_async_copy(
            g1blk.at[n], g1w.at[n, pl.ds(H1, X // 2), rows_c(0)], sem_loc.at[1 + n]
        )
        mine.start()
        mine.wait()
        each_c(n, lambda d: d.wait_recv(), -1)

        g1 = g1w.at[n]
        B1, B2 = X // 2, X // 4
        h8 = out0 + 3
        h4 = (h8 + 1) // 2
        h6 = h4 + 2
        h12 = 2 * h6
        apply(1, g1, g1, f1b, H1 - h12 - 2, H1 + B1 + h12 + 2)
        apply(1, f1b, g1, f1a, H1 - h12 - 1, H1 + B1 + h12 + 1)
        apply(1, f1a, g1, r1, H1 - h12, H1 + B1 + h12, residual=True)
        m = B2 + 2 * h6
        lo = H1 - h12
        half = [r1[lo + 2 * i] + r1[lo + 2 * i + 1] for i in range(m)]
        flat = 0.5 * dot(jnp.concatenate(half, axis=0), pz1)
        for i in range(m):
            g2[H2 - h6 + i] = dot(py1, flat[i * Y1 : (i + 1) * Y1])
        apply(2, g2, g2, f2b, H2 - h6 + 1, H2 + B2 + h6 - 1)
        apply(2, f2b, g2, f2a, H2 - h4, H2 + B2 + h4)
        m = B2 + 2 * h4
        flat = dot(jnp.concatenate([f2a[H2 - h4 + i] for i in range(m)], axis=0), uz1)
        for i in range(m):
            up = dot(uy1, flat[i * Y2 : (i + 1) * Y2])
            p = H1 - 2 * h4 + 2 * i
            f1a[p] = f1a[p] + up
            f1a[p + 1] = f1a[p + 1] + up
        apply(1, f1a, g1, f1b, H1 - out0 - 2, H1 + B1 + out0 + 2)
        apply(1, f1b, g1, f1a, H1 - out0 - 1, H1 + B1 + out0 + 1)
        apply(1, f1a, g1, f1b, H1 - out0, H1 + B1 + out0)
        m = B1 + 2 * out0
        flat = dot(jnp.concatenate([f1b[H1 - out0 + i] for i in range(m)], axis=0), uz0)
        for i in range(m):
            up = dot(uy0, flat[i * Y1 : (i + 1) * Y1])
            p = HALO0 - 2 * out0 + 2 * i
            src[p] = src[p] + up
            src[p + 1] = src[p + 1] + up

    def at(h):
        return HALO0 - h, HALO0 + X + h

    apply(0, gk, gk, fb, *at(11))
    apply(0, fb, gk, fa, *at(10))
    coarse(0, fa, 5)
    apply(0, fa, gk, fb, *at(9))
    apply(0, fb, gk, fa, *at(8))
    apply(0, fa, gk, fb, *at(7))
    apply(0, fb, gk, fa, *at(6))
    apply(0, fa, gk, fb, *at(5))
    apply(0, fb, gk, fa, *at(4))
    coarse(1, fa, 2)
    apply(0, fa, gk, fb, *at(3))
    apply(0, fb, gk, fa, *at(2))
    apply(0, fa, gk, fb, *at(1))

    acc = jnp.zeros((Y, Z), jnp.float32)
    r0, l0 = iotas((Y0, Z0))
    for i in range(X):
        p = HALO0 + i
        mid = fb[p]
        pot_ref[i] = own_lanes(own_rows(mid))
        j0 = 0.5 * own_lanes(own_rows(fb[p + 1] - fb[p - 1]))
        dy = jnp.where(r0 == Y0 - 1, 0.0, pltpu.roll(mid, Y0 - 1, 0)) - jnp.where(r0 == 0, 0.0, pltpu.roll(mid, 1, 0))
        dz = jnp.where(l0 == Z0 - 1, 0.0, pltpu.roll(mid, Z0 - 1, 1)) - jnp.where(l0 == 0, 0.0, pltpu.roll(mid, 1, 1))
        c0 = e_ref[0, i] - j0
        c1 = e_ref[1, i] - 0.5 * own_lanes(own_rows(dy))
        c2 = e_ref[2, i] - 0.5 * own_lanes(own_rows(dz))
        b0, b1, b2 = b_ref[0, i], b_ref[1, i], b_ref[2, i]
        m0 = v_ref[0, i] + section_weight * (c1 * b2 - c2 * b1)
        out_ref[0, i] = m0
        acc = acc + m0
        out_ref[1, i] = v_ref[1, i] + section_weight * (c2 * b0 - c0 * b2)
        out_ref[2, i] = v_ref[2, i] + section_weight * (c0 * b1 - c1 * b0)

    s1[...] = acc[:8] + acc[8:]
    pairs = [(dw, dt) for dw in range(CW) for dt in (0, 1)]

    def copy_p(k):
        dw, dt = pairs[k]
        return pltpu.make_async_remote_copy(
            s1, part1.at[k], sem_ps.at[k], sem_pr.at[k],
            device_id=(c, lax.rem(w + dw, CW), lax.rem(t + dt, 2)), device_id_type=MESH,
        )

    def copy_q(d):
        k = len(pairs) + d
        return pltpu.make_async_remote_copy(
            s2, part2.at[d], sem_ps.at[k], sem_pr.at[k],
            device_id=(lax.rem(c + d, CX), w, t), device_id_type=MESH,
        )

    for k in range(1, len(pairs)):
        copy_p(k).start()
    total = s1[...]
    for k in range(1, len(pairs)):
        copy_p(k).wait_recv()
        total = total + part1[k]
    s2[...] = total
    for d in range(1, CX):
        copy_q(d).start()
    for d in range(1, CX):
        copy_q(d).wait_recv()
        total = total + part2[d]
    bulk = jnp.sum(total) * (1.0 / float(nx0 * CW * Y * Z0))
    for i in range(X):
        out_ref[0, i] = out_ref[0, i] - bulk + cast_speed

    for k in range(4):
        pl.when(send_ok[k])(lambda k=k: copy_a(k).wait_send())
    copy_a(4).wait_send()
    each_b(lambda d: d.wait_send(), 1)
    for n in range(CYCLES):
        each_c(n, lambda d: d.wait_send(), 1)
    for k in range(1, len(pairs)):
        copy_p(k).wait_send()
    for d in range(1, CX):
        copy_q(d).wait_send()


def solution(mesh):
    CX, CW = mesh.shape["cast"], mesh.shape["width"]

    def per_device(velocity, magnetic):
        _, X, Y, Z = velocity.shape
        two = CW == 2
        Y0 = 2 * Y if two else 3 * Y
        Y1 = Y if two else 5 * (Y // 2)
        Y2 = -(-(Y1 // 2) // 8) * 8
        Z0 = 2 * Z
        N0, N1, N2 = X + 2 * HALO0, (X // 2) * (2 * NEAR + 1), (X // 4) * (2 * NEAR + 1)
        nb, nc = 5 * (2 if two else 3) * 2, (2 * NEAR + 1) * (2 if two else 5)
        np_ = 2 * CW + CX
        f32 = jnp.float32
        V = pltpu.VMEM
        D = pltpu.SemaphoreType.DMA
        return pl.pallas_call(
            functools.partial(kernel, (CX, CW)),
            out_shape=(
                jax.ShapeDtypeStruct((3, X, Y, Z), f32),
                jax.ShapeDtypeStruct((X, Y, Z), f32),
            ),
            in_specs=[pl.BlockSpec(memory_space=V)] * 2,
            out_specs=(pl.BlockSpec(memory_space=V),) * 2,
            scratch_shapes=[
                V((3, X, Y, Z), f32), V((X, Y, Z), f32), V((Y, Z), f32), V((Y, Z), f32),
                V((2, X, Z), f32), V((2, X, Z), f32), V((X, Y, Z), f32),
                V((N0, Y0, Z0), f32), V((N0, Y0, Z0), f32), V((N0, Y0, Z0), f32),
                V((CYCLES, X // 2, Y // 2, Z), f32), V((CYCLES, N1, Y1, Z), f32),
                V((N1, Y1, Z), f32), V((N1, Y1, Z), f32), V((N1, Y1, Z), f32),
                V((N2, Y2, Z), f32), V((N2, Y2, Z), f32), V((N2, Y2, Z), f32),
                V((8, Z), f32), V((8, Z), f32), V((2 * CW, 8, Z), f32), V((CX, 8, Z), f32),
                D((5,)), D((5,)), D((nb,)), D((nb,)), D((CYCLES, nc)), D((CYCLES, nc)),
                D((np_,)), D((np_,)), D((1 + CYCLES,)),
            ],
            compiler_params=pltpu.CompilerParams(
                collective_id=0, has_side_effects=True, vmem_limit_bytes=40 * 1024 * 1024
            ),
        )(velocity, magnetic)

    placed = (P(None, "cast", "width", "thick"), P(None, "cast", "width", "thick"))
    return jax.shard_map(
        per_device,
        mesh=mesh,
        in_specs=placed,
        out_specs=(P(None, "cast", "width", "thick"), P("cast", "width", "thick")),
        check_vma=False,
    )
```

time: 771 us -> 72.1 us (0.09)
  starting transfers between devices: 551 us -> 0 us
  waiting for transfers between devices: 134 us -> 0 us
  Pallas kernels: 0 us -> 68.1 us
  blocking collectives: 45.9 us -> 0 us
  local copies, waits for them, and re-layouts: 16.8 us -> 3.15 us
  other arithmetic: 12.8 us -> 0 us
    ppermute x204 -> x0, starting transfers between devices: 551 us -> none  [the longest x102 419 us: padded_2(): lax.ppermute(lax.slice_in_dim(block, block.shape[dim] - width, None, axis...]
    ppermute x204 -> x0, waiting for transfers between devices: 134 us -> none  [the longest x102 84.3 us: padded_2(): lax.ppermute(lax.slice_in_dim(block, block.shape[dim] - width, None, axis...]
    pallas_call x0 -> x1, Pallas kernels: none -> 68.1 us  [per_device(): pl.pallas_call(functools.partial(kernel, (CX, CW)), out_shape=(jax.ShapeD...]
    psum x1 -> x0, blocking collectives: 45.9 us -> none  [per_device(): total = lax.psum(jnp.sum(moved[0]), ('cast', 'width', 'thick'))]
    reshape x12 -> x0, local copies, waits for them, and re-layouts: 13.2 us -> none  [the longest x4 12.2 us: restrict(): blocks = residue.reshape(count_x // 2, 2, count_y // 2, 2, count_z // 2, 2)]
  transfers between devices with their start and end apart: 204 -> 0, of which waited for: 86 -> 0; matrix products, arithmetic and copies ran while one was open for 0% -> 0% of each run, Pallas kernels for 0% -> 0%
where the time goes in v1:
time: 72.1 us; the launch traced here: 71.9 us
  Pallas kernels  68.1 us (94%)
  local copies, waits for them, and re-layouts  3.15 us (4%)
    pallas_call x1, Pallas kernels, per_device(): pl.pallas_call(functools.partial(kernel, (CX, CW)), out_shape=(jax.ShapeD...  68.1 us
    unnamed x6, local copies, waits for them, and re-layouts  3.15 us

profile of v1, /device:TPU:0, one launch (start us, length us, event | category | flops | bytes accessed | tf_op | source)
XLA Modules:
  0.0 71.9 jit_solution(14580569532834890691)
XLA Ops:
  0.6 0.0 copy-start
  0.6 0.9 %copy-done = f32[3,8,16,128]{3,2,1,0:T(8,128)S(1)} copy-done((f32[3,8,16,128]{3,2,1,0:T(8,128)S(1)}, f32[3,8,16,128]{3,2,1,0:T(8,128)}, u32[]{:S(2)}) %copy-start) | copy-done | bytes 196632
  1.6 0.0 copy-start.1
  1.6 0.9 %copy-done.1 = f32[3,8,16,128]{3,2,1,0:T(8,128)S(1)} copy-done((f32[3,8,16,128]{3,2,1,0:T(8,128)S(1)}, f32[3,8,16,128]{3,2,1,0:T(8,128)}, u32[]{:S(2)}) %copy-start.1) | copy-done | bytes 196632
  2.5 68.1 %shard_map.41 = (f32[3,8,16,128]{3,2,1,0:T(8,128)S(1)}, f32[8,16,128]{2,1,0:T(8,128)S(1)}) custom-call(f32[3,8,16,128]{3,2,1,0:T(8,128)S(1)} %copy-done, f32[3,8,16,128]{3,2,1,0:T(8,128)S(1)} %copy-done.1), custom_call_target="tpu_custom_call" | custom-call | tf_op jit(solution)/shard_map/pallas_call | solution.py:472
  70.6 0.7 copy.6
  71.3 0.6 copy.7
Async XLA Ops:
  0.6 0.9 %copy-start = (f32[3,8,16,128]{3,2,1,0:T(8,128)S(1)}, f32[3,8,16,128]{3,2,1,0:T(8,128)}, u32[]{:S(2)}) copy-start(f32[3,8,16,128]{3,2,1,0:T(8,128)} %v_ref.1) | copy-start | bytes 589828
  1.6 0.9 %copy-start.1 = (f32[3,8,16,128]{3,2,1,0:T(8,128)S(1)}, f32[3,8,16,128]{3,2,1,0:T(8,128)}, u32[]{:S(2)}) copy-start(f32[3,8,16,128]{3,2,1,0:T(8,128)} %b_ref.1) | copy-start | bytes 589828

commit v2 on v1

--- a/solution.py
+++ b/solution.py
@@ -12,15 +12,26 @@
 keep = 0.2
 section_weight = 0.5
 cast_speed = 1.0
-HIGH = lax.Precision.HIGHEST
 MESH = pl.DeviceIdType.MESH
 
 HALO0 = 12
 NEAR = 4
 
 
+def pieces(a):
+    high = a.astype(jnp.bfloat16)
+    rest = a - high.astype(jnp.float32)
+    mid = rest.astype(jnp.bfloat16)
+    low = (rest - mid.astype(jnp.float32)).astype(jnp.bfloat16)
+    return high, mid, low
+
+
 def dot(a, b):
-    return jnp.dot(a, b, precision=HIGH, preferred_element_type=jnp.float32)
+    if a.dtype == jnp.bfloat16:
+        parts = [jnp.dot(a, q, preferred_element_type=jnp.float32) for q in pieces(b)]
+    else:
+        parts = [jnp.dot(q, b, preferred_element_type=jnp.float32) for q in pieces(a)]
+    return parts[0] + (parts[1] + parts[2])
 
 
 def iotas(shape):
@@ -33,7 +44,7 @@
         hit = lax.shift_right_logical(i, 1) + offset == j
     else:
         hit = lax.shift_right_logical(j, 1) == i
-    return jnp.where(hit, 1.0, 0.0).astype(jnp.float32)
+    return jnp.where(hit, 1.0, 0.0).astype(jnp.bfloat16)
 
 
 def kernel(
@@ -86,30 +97,7 @@
 
         lax.fori_loop(0, count // per, body, 0)
 
-    if two:
-        @pl.when(jnp.logical_not(has_x(-2)))
-        def _():
-            clear(gk, 0, 4, 4)
-
-        @pl.when(jnp.logical_not(has_x(-1)))
-        def _():
-            clear(gk, 4, 8, 4)
-
-        @pl.when(jnp.logical_not(has_x(1)))
-        def _():
-            clear(gk, 20, 8, 4)
-
-        @pl.when(jnp.logical_not(has_x(2)))
-        def _():
-            clear(gk, 28, 4, 4)
-
-        for n in range(CYCLES):
-            for dx in range(-NEAR, NEAR + 1):
-                if dx:
-                    @pl.when(jnp.logical_not(has_x(dx)))
-                    def _(n=n, dx=dx):
-                        clear(g1w.at[n], 4 * (NEAR + dx), 4, 4)
-    else:
+    if not two:
         clear(gk, 0, gk.shape[0], 4)
         for n in range(CYCLES):
             clear(g1w.at[n], 0, g1w.shape[1], 4)
@@ -125,9 +113,8 @@
             for dt in (0, 1):
                 if dy == 0 and dt == 0:
                     continue
-                wide = abs(dx) <= 2 and (two or abs(dy) <= 1)
-                coarse = dt == 0 and (two or abs(dy) <= 2)
-                if not (wide or coarse or dx == 0):
+                near = dt == 0 and (two or abs(dy) <= 2)
+                if not (near or dx == 0):
                     continue
                 ok = jnp.bool_(True)
                 if dx:
@@ -146,6 +133,30 @@
                 else:
                     pl.when(ok)(greet)
                     need = need + jnp.where(ok, 1, 0).astype(jnp.int32)
+
+    if two:
+        @pl.when(jnp.logical_not(has_x(-2)))
+        def _():
+            clear(gk, 0, 4, 4)
+
+        @pl.when(jnp.logical_not(has_x(-1)))
+        def _():
+            clear(gk, 4, 8, 4)
+
+        @pl.when(jnp.logical_not(has_x(1)))
+        def _():
+            clear(gk, 20, 8, 4)
+
+        @pl.when(jnp.logical_not(has_x(2)))
+        def _():
+            clear(gk, 28, 4, 4)
+
+        for n in range(CYCLES):
+            for dx in range(-NEAR, NEAR + 1):
+                if dx:
+                    @pl.when(jnp.logical_not(has_x(dx)))
+                    def _(n=n, dx=dx):
+                        clear(g1w.at[n], 4 * (NEAR + dx), 4, 4)
 
     for i in range(X):
         v0, v1, v2 = v_ref[0, i], v_ref[1, i], v_ref[2, i]
@@ -201,46 +212,74 @@
 
     my_lanes = pl.ds(pl.multiple_of(t * Z, Z), Z)
     ydys = dys(1)
-
-    def copy_b(dx, dy, dt):
-        if dx == 2:
-            src, dst = (4, 4), 0
-        elif dx == -2:
-            src, dst = (0, 4), HALO0 + X + X
-        else:
-            src, dst = (0, X), HALO0 - dx * X
-        k = ((dx + 2) * len(ydys) + ydys.index(dy)) * 2 + dt
-        return pltpu.make_async_remote_copy(
-            sblk.at[pl.ds(src[0], src[1])],
-            gk.at[pl.ds(dst, src[1]), rows_b(dy), my_lanes],
-            sem_bs.at[k], sem_br.at[k],
-            device_id=(c + dx, wid(dy), lax.rem(t + dt, 2)), device_id_type=MESH,
-        )
-
-    def each_b(fn, sign):
-        for dx in (1, -1, 2, -2, 0):
-            def run(dx=dx):
+    other = (c, w, 1 - t)
+    mid = [(0, 0, X, HALO0)]
+    near = mid + [(1, X - 4, 4, HALO0 - 4), (-1, 0, 4, HALO0 + X)]
+    far = [
+        (1, 0, 4, HALO0 - 8), (-1, X - 4, 4, HALO0 + X + 4),
+        (2, X - 4, 4, HALO0 - 12), (-2, 0, 4, HALO0 + X + 8),
+    ]
+    steps = near + far
+
+    def slot_b(entry, dy):
+        return steps.index(entry) * len(ydys) + ydys.index(dy)
+
+    def rows_in(dy, size, reach):
+        return pl.ds(pl.multiple_of(wid(dy) * size, size), size) if two else pl.ds((reach - dy) * size, size)
+
+    def copy_b(entry, dy):
+        dx, first, count, land = entry
+        k = slot_b(entry, dy)
+        return pltpu.make_async_remote_copy(
+            sblk.at[pl.ds(first, count)],
+            gk.at[pl.ds(land, count), rows_b(dy), my_lanes],
+            sem_bs.at[0, k], sem_br.at[0, k],
+            device_id=(c + dx, wid(dy), t), device_id_type=MESH,
+        )
+
+    def pass_b(entry, dy):
+        _, _, count, land = entry
+        k = slot_b(entry, dy)
+        place = gk.at[pl.ds(land, count), rows_in(dy, Y, 1), my_lanes]
+        src = sblk if entry[0] == 0 and dy == 0 else place
+        return pltpu.make_async_remote_copy(
+            src, place, sem_bs.at[1, k], sem_br.at[1, k], device_id=other, device_id_type=MESH
+        )
+
+    def each_b(entries, fn, sign):
+        for entry in entries:
+            def run(entry=entry):
                 for dy in ydys:
-                    def run_w(dy=dy):
-                        for dt in (0, 1):
-                            if dx or dy or dt:
-                                fn(copy_b(dx, dy, dt))
-
-                    if two:
-                        run_w()
-                    else:
-                        when_w(sign * dy, run_w)
-
-            when_x(sign * dx, run)
-
-    each_b(lambda d: d.start(), 1)
+                    when_w(sign * dy, lambda dy=dy: fn(entry, dy))
+
+            when_x(sign * entry[0], run)
+
+    def is_own(entry, dy):
+        return entry[0] == 0 and dy == 0
+
+    def start_b(entry, dy):
+        if not is_own(entry, dy):
+            copy_b(entry, dy).start()
+
+    def hand_on(entry, dy):
+        if not is_own(entry, dy):
+            copy_b(entry, dy).wait_recv()
+            pass_b(entry, dy).start()
+
+    def leave_b(entry, dy):
+        if not is_own(entry, dy):
+            copy_b(entry, dy).wait_send()
+
+    each_b(steps, start_b, 1)
+    pass_b(mid[0], 0).start()
     own = pltpu.make_async_copy(
         sblk, gk.at[pl.ds(HALO0, X), pl.ds(pl.multiple_of(w * Y, Y), Y) if two else pl.ds(Y, Y), my_lanes],
         sem_loc.at[0],
     )
     own.start()
     own.wait()
-    each_b(lambda d: d.wait_recv(), -1)
+    each_b(near, hand_on, -1)
+    each_b(near, lambda entry, dy: pass_b(entry, dy).wait_recv(), -1)
 
     def neighbours(v):
         ny, nz = v.shape
@@ -266,7 +305,7 @@
         first = (c * X - HALO0, c * (X // 2) - NEAR * (X // 2), c * (X // 4) - NEAR * (X // 4))[lev]
         count = nx0 >> lev
         n = hi - lo
-        step = max(d for d in ((1, 2) if lev == 0 else (1, 2, 3, 4, 5)) if n % d == 0)
+        step = max(d for d in ((1, 2, 3, 4, 5) if lev == 0 else (1, 2, 3, 4, 5, 6, 7, 8)) if n % d == 0)
 
         def body(i, carry):
             p = lo + i * step
@@ -306,36 +345,54 @@
         half = Y // 2
         return pl.ds(pl.multiple_of(w * half, half), half) if two else pl.ds((2 - dy) * half, half)
 
+    part = X // 4
+
     def copy_c(n, dx, dy):
         k = (dx + NEAR) * len(cdys) + cdys.index(dy)
         return pltpu.make_async_remote_copy(
-            g1blk.at[n], g1w.at[n, pl.ds((NEAR - dx) * (X // 2), X // 2), rows_c(dy)],
-            sem_cs.at[n, k], sem_cr.at[n, k],
+            g1blk.at[n, pl.ds(t * part, part)],
+            g1w.at[n, pl.ds((NEAR - dx) * (X // 2) + t * part, part), rows_c(dy)],
+            sem_cs.at[n, 0, k], sem_cr.at[n, 0, k],
             device_id=(c + dx, wid(dy), t), device_id_type=MESH,
         )
 
-    def each_c(n, fn, sign):
-        for dx in (4, -4, 3, -3, 2, -2, 1, -1, 0):
+    def pass_c(n, dx, dy):
+        k = (dx + NEAR) * len(cdys) + cdys.index(dy)
+        place = g1w.at[n, pl.ds((NEAR - dx) * (X // 2) + t * part, part), rows_in(dy, Y // 2, 2)]
+        return pltpu.make_async_remote_copy(
+            place, place, sem_cs.at[n, 1, k], sem_cr.at[n, 1, k], device_id=other, device_id_type=MESH
+        )
+
+    def each_c(n, fn, sign, order):
+        for dx in order:
             def run(dx=dx):
                 for dy in cdys:
                     if dx or dy:
-                        when_w(sign * dy, lambda dy=dy: fn(copy_c(n, dx, dy)))
+                        when_w(sign * dy, lambda dy=dy: fn(n, dx, dy))
 
             when_x(sign * dx, run)
 
-    def coarse(n, src, out0):
+    outward = (0, 1, -1, 2, -2, 3, -3, 4, -4)
+
+    def hand_on_c(n, dx, dy):
+        copy_c(n, dx, dy).wait_recv()
+        pass_c(n, dx, dy).start()
+
+    def coarse(n, src, out0, between):
         apply(0, src, gk, fb, HALO0, HALO0 + X, residual=True)
         sums = [own_rows(fb[HALO0 + 2 * i] + fb[HALO0 + 2 * i + 1]) for i in range(X // 2)]
         flat = 0.5 * dot(jnp.concatenate(sums, axis=0), pz0)
         for i in range(X // 2):
             g1blk[n, i] = dot(py0, flat[i * Y : (i + 1) * Y])
-        each_c(n, lambda d: d.start(), 1)
+        each_c(n, lambda *a: copy_c(*a).start(), 1, outward[::-1])
         mine = pltpu.make_async_copy(
             g1blk.at[n], g1w.at[n, pl.ds(H1, X // 2), rows_c(0)], sem_loc.at[1 + n]
         )
         mine.start()
         mine.wait()
-        each_c(n, lambda d: d.wait_recv(), -1)
+        between()
+        each_c(n, hand_on_c, -1, outward)
+        each_c(n, lambda *a: pass_c(*a).wait_recv(), -1, outward)
 
         g1 = g1w.at[n]
         B1, B2 = X // 2, X // 4
@@ -375,16 +432,25 @@
     def at(h):
         return HALO0 - h, HALO0 + X + h
 
-    apply(0, gk, gk, fb, *at(11))
-    apply(0, fb, gk, fa, *at(10))
-    coarse(0, fa, 5)
+    def rest():
+        each_b(far, hand_on, -1)
+        each_b(far, lambda entry, dy: pass_b(entry, dy).wait_recv(), -1)
+        low, high = HALO0, HALO0 + X
+        apply(0, gk, gk, fb, low - 11, low - 2)
+        apply(0, gk, gk, fb, high + 2, high + 11)
+        apply(0, fb, gk, fa, low - 10, low - 1)
+        apply(0, fb, gk, fa, high + 1, high + 10)
+
+    apply(0, gk, gk, fb, *at(2))
+    apply(0, fb, gk, fa, *at(1))
+    coarse(0, fa, 5, rest)
     apply(0, fa, gk, fb, *at(9))
     apply(0, fb, gk, fa, *at(8))
     apply(0, fa, gk, fb, *at(7))
     apply(0, fb, gk, fa, *at(6))
     apply(0, fa, gk, fb, *at(5))
     apply(0, fb, gk, fa, *at(4))
-    coarse(1, fa, 2)
+    coarse(1, fa, 2, lambda: None)
     apply(0, fa, gk, fb, *at(3))
     apply(0, fb, gk, fa, *at(2))
     apply(0, fa, gk, fb, *at(1))
@@ -444,9 +510,11 @@
     for k in range(4):
         pl.when(send_ok[k])(lambda k=k: copy_a(k).wait_send())
     copy_a(4).wait_send()
-    each_b(lambda d: d.wait_send(), 1)
+    each_b(steps, leave_b, 1)
+    each_b(steps, lambda entry, dy: pass_b(entry, dy).wait_send(), -1)
     for n in range(CYCLES):
-        each_c(n, lambda d: d.wait_send(), 1)
+        each_c(n, lambda *a: copy_c(*a).wait_send(), 1, outward)
+        each_c(n, lambda *a: pass_c(*a).wait_send(), -1, outward)
     for k in range(1, len(pairs)):
         copy_p(k).wait_send()
     for d in range(1, CX):
@@ -464,7 +532,7 @@
         Y2 = -(-(Y1 // 2) // 8) * 8
         Z0 = 2 * Z
         N0, N1, N2 = X + 2 * HALO0, (X // 2) * (2 * NEAR + 1), (X // 4) * (2 * NEAR + 1)
-        nb, nc = 5 * (2 if two else 3) * 2, (2 * NEAR + 1) * (2 if two else 5)
+        nb, nc = 7 * (2 if two else 3), (2 * NEAR + 1) * (2 if two else 5)
         np_ = 2 * CW + CX
         f32 = jnp.float32
         V = pltpu.VMEM
@@ -485,7 +553,7 @@
                 V((N1, Y1, Z), f32), V((N1, Y1, Z), f32), V((N1, Y1, Z), f32),
                 V((N2, Y2, Z), f32), V((N2, Y2, Z), f32), V((N2, Y2, Z), f32),
                 V((8, Z), f32), V((8, Z), f32), V((2 * CW, 8, Z), f32), V((CX, 8, Z), f32),
-                D((5,)), D((5,)), D((nb,)), D((nb,)), D((CYCLES, nc)), D((CYCLES, nc)),
+                D((5,)), D((5,)), D((2, nb)), D((2, nb)), D((CYCLES, 2, nc)), D((CYCLES, 2, nc)),
                 D((np_,)), D((np_,)), D((1 + CYCLES,)),
             ],
             compiler_params=pltpu.CompilerParams(

time: 72.1 us -> 57.5 us (0.80)
  Pallas kernels: 68.1 us -> 53.6 us
    pallas_call x1, Pallas kernels: 68.1 us -> 53.6 us  [per_device(): pl.pallas_call(functools.partial(kernel, (CX, CW)), out_shape=(jax.ShapeD...]
where the time goes in v2:
time: 57.5 us; the launch traced here: 57.4 us
  Pallas kernels  53.6 us (93%)
  local copies, waits for them, and re-layouts  3.15 us (5%)
  between operations  0.65 us (1%)
    pallas_call x1, Pallas kernels, per_device(): pl.pallas_call(functools.partial(kernel, (CX, CW)), out_shape=(jax.ShapeD...  53.6 us
    unnamed x6, local copies, waits for them, and re-layouts  3.15 us

profile of v2, /device:TPU:0, one launch (start us, length us, event | category | flops | bytes accessed | tf_op | source)
XLA Modules:
  0.0 57.4 jit_solution(6285257270883300837)
XLA Ops:
  0.6 0.0 copy-start
  0.6 0.9 %copy-done = f32[3,8,16,128]{3,2,1,0:T(8,128)S(1)} copy-done((f32[3,8,16,128]{3,2,1,0:T(8,128)S(1)}, f32[3,8,16,128]{3,2,1,0:T(8,128)}, u32[]{:S(2)}) %copy-start) | copy-done | bytes 196632
  1.6 0.0 copy-start.1
  1.6 0.9 %copy-done.1 = f32[3,8,16,128]{3,2,1,0:T(8,128)S(1)} copy-done((f32[3,8,16,128]{3,2,1,0:T(8,128)S(1)}, f32[3,8,16,128]{3,2,1,0:T(8,128)}, u32[]{:S(2)}) %copy-start.1) | copy-done | bytes 196632
  2.5 53.6 %shard_map.41 = (f32[3,8,16,128]{3,2,1,0:T(8,128)S(1)}, f32[8,16,128]{2,1,0:T(8,128)S(1)}) custom-call(f32[3,8,16,128]{3,2,1,0:T(8,128)S(1)} %copy-done, f32[3,8,16,128]{3,2,1,0:T(8,128)S(1)} %copy-done.1), custom_call_target="tpu_custom_call" | custom-call | tf_op jit(solution)/shard_map/pallas_call | solution.py:540
  56.1 0.7 %copy.6 = f32[3,8,16,128]{3,2,1,0:T(8,128)} copy(f32[3,8,16,128]{3,2,1,0:T(8,128)S(1)} %get-tuple-element.4) | data formatting | bytes 393216
  56.7 0.6 %copy.7 = f32[8,16,128]{2,1,0:T(8,128)} copy(f32[8,16,128]{2,1,0:T(8,128)S(1)} %get-tuple-element.5) | data formatting | bytes 131072
Async XLA Ops:
  0.6 0.9 %copy-start = (f32[3,8,16,128]{3,2,1,0:T(8,128)S(1)}, f32[3,8,16,128]{3,2,1,0:T(8,128)}, u32[]{:S(2)}) copy-start(f32[3,8,16,128]{3,2,1,0:T(8,128)} %v_ref.1) | copy-start | bytes 589828
  1.6 0.9 %copy-start.1 = (f32[3,8,16,128]{3,2,1,0:T(8,128)S(1)}, f32[3,8,16,128]{3,2,1,0:T(8,128)}, u32[]{:S(2)}) copy-start(f32[3,8,16,128]{3,2,1,0:T(8,128)} %b_ref.1) | copy-start | bytes 589828

commit v3 on v2

--- a/solution.py
+++ b/solution.py
@@ -305,7 +305,7 @@
         first = (c * X - HALO0, c * (X // 2) - NEAR * (X // 2), c * (X // 4) - NEAR * (X // 4))[lev]
         count = nx0 >> lev
         n = hi - lo
-        step = max(d for d in ((1, 2, 3, 4, 5) if lev == 0 else (1, 2, 3, 4, 5, 6, 7, 8)) if n % d == 0)
+        step = max(d for d in range(1, 14 if lev == 0 else 18) if n % d == 0)
 
         def body(i, carry):
             p = lo + i * step
@@ -447,10 +447,16 @@
     apply(0, fa, gk, fb, *at(9))
     apply(0, fb, gk, fa, *at(8))
     apply(0, fa, gk, fb, *at(7))
-    apply(0, fb, gk, fa, *at(6))
-    apply(0, fa, gk, fb, *at(5))
-    apply(0, fb, gk, fa, *at(4))
-    coarse(1, fa, 2, lambda: None)
+    def outer():
+        low, high = HALO0, HALO0 + X
+        for src, dst, h in ((fb, fa, 6), (fa, fb, 5), (fb, fa, 4)):
+            apply(0, src, gk, dst, low - h, low - h + 3)
+            apply(0, src, gk, dst, high + h - 3, high + h)
+
+    apply(0, fb, gk, fa, *at(3))
+    apply(0, fa, gk, fb, *at(2))
+    apply(0, fb, gk, fa, *at(1))
+    coarse(1, fa, 2, outer)
     apply(0, fa, gk, fb, *at(3))
     apply(0, fb, gk, fa, *at(2))
     apply(0, fa, gk, fb, *at(1))

time: 57.5 us -> 50.6 us (0.88)
  Pallas kernels: 53.6 us -> 46.7 us
    pallas_call x1, Pallas kernels: 53.6 us -> 46.7 us  [per_device(): pl.pallas_call(functools.partial(kernel, (CX, CW)), out_shape=(jax.ShapeD...]
where the time goes in v3:
time: 50.6 us; the launch traced here: 50.5 us
  Pallas kernels  46.7 us (92%)
  local copies, waits for them, and re-layouts  3.15 us (6%)
  between operations  0.65 us (1%)
    pallas_call x1, Pallas kernels, per_device(): pl.pallas_call(functools.partial(kernel, (CX, CW)), out_shape=(jax.ShapeD...  46.7 us
    unnamed x6, local copies, waits for them, and re-layouts  3.15 us

profile of v3, /device:TPU:0, one launch (start us, length us, event | category | flops | bytes accessed | tf_op | source)
XLA Modules:
  0.0 50.5 jit_solution(17604136271627609939)
XLA Ops:
  0.6 0.0 copy-start
  0.6 0.9 %copy-done = f32[3,8,16,128]{3,2,1,0:T(8,128)S(1)} copy-done((f32[3,8,16,128]{3,2,1,0:T(8,128)S(1)}, f32[3,8,16,128]{3,2,1,0:T(8,128)}, u32[]{:S(2)}) %copy-start) | copy-done | bytes 196632
  1.6 0.0 copy-start.1
  1.6 0.9 %copy-done.1 = f32[3,8,16,128]{3,2,1,0:T(8,128)S(1)} copy-done((f32[3,8,16,128]{3,2,1,0:T(8,128)S(1)}, f32[3,8,16,128]{3,2,1,0:T(8,128)}, u32[]{:S(2)}) %copy-start.1) | copy-done | bytes 196632
  2.5 46.7 %shard_map.41 = (f32[3,8,16,128]{3,2,1,0:T(8,128)S(1)}, f32[8,16,128]{2,1,0:T(8,128)S(1)}) custom-call(f32[3,8,16,128]{3,2,1,0:T(8,128)S(1)} %copy-done, f32[3,8,16,128]{3,2,1,0:T(8,128)S(1)} %copy-done.1), custom_call_target="tpu_custom_call" | custom-call | tf_op jit(solution)/shard_map/pallas_call | solution.py:546
  49.2 0.7 %copy.6 = f32[3,8,16,128]{3,2,1,0:T(8,128)} copy(f32[3,8,16,128]{3,2,1,0:T(8,128)S(1)} %get-tuple-element.4) | data formatting | bytes 393216
  49.8 0.6 %copy.7 = f32[8,16,128]{2,1,0:T(8,128)} copy(f32[8,16,128]{2,1,0:T(8,128)S(1)} %get-tuple-element.5) | data formatting | bytes 131072
Async XLA Ops:
  0.6 0.9 %copy-start = (f32[3,8,16,128]{3,2,1,0:T(8,128)S(1)}, f32[3,8,16,128]{3,2,1,0:T(8,128)}, u32[]{:S(2)}) copy-start(f32[3,8,16,128]{3,2,1,0:T(8,128)} %v_ref.1) | copy-start | bytes 589828
  1.6 0.9 %copy-start.1 = (f32[3,8,16,128]{3,2,1,0:T(8,128)S(1)}, f32[3,8,16,128]{3,2,1,0:T(8,128)}, u32[]{:S(2)}) copy-start(f32[3,8,16,128]{3,2,1,0:T(8,128)} %b_ref.1) | copy-start | bytes 589828
